TPU v7x, 32 devices: a whole 2x2x4 slice. The times are simulated.
32 devices in a mesh: parts: 2 (over y), label: 16 (over z, x, core), doc: 1.
Axes of the slice: x: 2, y: 2, z: 4, core: 2. Of those that a mesh axis runs over, the one named last changes fastest.
Arguments:
- features: bfloat16 [4096, 768], P(('parts', 'label', 'doc')), parts along dimension 0, may hold values from -6 to 6
- w_encoder: bfloat16 [768, 768], P('label'), may hold values from -0.21875 to 0.21875
- norm_gain: float32 [768], replicated, may hold values from 0.25 to 1.75
- label_table: bfloat16 [128, 128, 768], P(('parts', 'label')), parts along dimension 0, may hold values from -0.21875 to 0.21875
- block_place: int32 [128], P('parts'), parts along dimension 0, may hold values from 0 to 63, as said below
- beams: int32 [4096, 2], P(('parts', 'label', 'doc')), parts along dimension 0, may hold values from -1 to 63, as said below
- positives: int32 [4096, 4], P(('parts', 'label', 'doc')), parts along dimension 0, may hold values from 0 to 8191
Outputs:
- doc_grad: bfloat16 [4096, 768], P(('parts', 'label', 'doc')), parts along dimension 0
- label_grad: float32 [128, 128, 768], P(('parts', 'label'), 'doc'), parts along dimension 0
There are 2 independent parts, one for each index of `parts`. A program takes and returns all parts, laid end to end along the dimension named above; an argument that names none is the same for every part. Nothing has to cross between parts.
Inputs may be any that keep to these rules, and one draw needn't show every extreme that they name: `block_place`: A permutation: each block has its own row. `beams`: entries are block ids or -1 for padding. Among the beam slots of the 128 documents of one device (aligned blocks of rows), at most 8 name any one block; on some device every block held by some label shard is named by exactly 8 of them.
All inputs are finite; a program needn't handle non-finite values.
Results may differ from a plain program's by a relative error of at most 0.015.
Values may be sent and summed in bfloat16 or wider, within the bound.
A program may use at most 64 MiB of HBM per device.

v0:
```python
import jax
import jax.numpy as jnp
from jax import lax
from jax.sharding import PartitionSpec as P

hinge_weight = 0.125


def coefficients(entry_emb, entry_info, table_blocks):
    label_span = table_blocks.shape[1]
    scores = jnp.einsum("bcd,bjd->bcj", entry_emb, table_blocks, preferred_element_type=jnp.float32)
    positions = jnp.arange(label_span, dtype=jnp.int32)
    matched = jnp.any(entry_info[:, :, 1:, None] == positions[None, None, None, :], axis=2)
    signs = jnp.where(matched, 1.0, -1.0).astype(jnp.float32)
    valid = entry_info[:, :, 0:1] > 0
    raw_coef = jnp.where(
        valid, -2.0 * hinge_weight * signs * jnp.maximum(0.0, 1.0 - signs * scores), 0.0
    )
    return raw_coef.astype(jnp.bfloat16)


def local(features, w_encoder, norm_gain, label_table, block_place, beams, positives):
    doc_total, width = features.shape
    blocks_here = label_table.shape[0]
    block_size = label_table.shape[1]
    label_shards = lax.axis_size("label")
    encoded = jnp.dot(
        features,
        lax.all_gather(w_encoder, "label", axis=0, tiled=True),
        preferred_element_type=jnp.float32,
    )
    scale_rows = lax.rsqrt(jnp.mean(encoded * encoded, axis=-1, keepdims=True) + 1e-06)
    embedded = (encoded * scale_rows * norm_gain).astype(jnp.bfloat16)
    beam_width = beams.shape[1]
    slot_total = doc_total * beam_width
    total_blocks = blocks_here * label_shards
    capacity = max(2, 2 * slot_total // total_blocks)
    buffer_size = total_blocks * capacity
    present = beams >= 0
    block_ids = jnp.where(present, beams, 0)
    table_rows = block_place[block_ids].reshape(-1)
    present_flat = present.reshape(-1)
    row_hits = (
        (table_rows[:, None] == jnp.arange(total_blocks, dtype=jnp.int32)[None, :])
        & present_flat[:, None]
    ).astype(jnp.int32)
    ranks = jnp.sum((jnp.cumsum(row_hits, axis=0) - row_hits) * row_hits, axis=1)
    slot_target = jnp.where(present_flat, table_rows * capacity + ranks, buffer_size)
    source_docs = (
        jnp.zeros((buffer_size,), jnp.int32)
        .at[slot_target]
        .set(jnp.arange(slot_total, dtype=jnp.int32) // beam_width, mode="drop")
    )
    occupied = jnp.zeros((buffer_size,), jnp.bool_).at[slot_target].set(True, mode="drop")
    outgoing = jnp.where(occupied[:, None], embedded[source_docs], jnp.zeros((), jnp.bfloat16))
    outgoing = outgoing.reshape(label_shards, blocks_here, capacity, width)
    offsets = positives[:, None, :] - block_ids[:, :, None] * block_size
    offsets = jnp.where(present[:, :, None] & (offsets >= 0) & (offsets < block_size), offsets, -1)
    slot_info = jnp.concatenate(
        [jnp.ones((slot_total, 1), jnp.int32), offsets.reshape(slot_total, -1)], axis=1
    )
    info_buffer = (
        jnp.zeros((buffer_size, slot_info.shape[1]), jnp.int32)
        .at[slot_target]
        .set(slot_info, mode="drop")
    )
    info_buffer = info_buffer.reshape(label_shards, blocks_here, capacity, -1)
    arrived, arrived_info = (
        lax.all_to_all(outgoing, "label", split_axis=0, concat_axis=2, tiled=True),
        lax.all_to_all(info_buffer, "label", split_axis=0, concat_axis=2, tiled=True),
    )
    entry_count = label_shards * capacity
    arrived = arrived.reshape(blocks_here, entry_count, width)
    arrived_info = arrived_info.reshape(blocks_here, entry_count, -1)
    coef = coefficients(arrived, arrived_info, label_table)
    replies = jnp.einsum(
        "bcj,bjd->bcd", coef, label_table, preferred_element_type=jnp.float32
    ).astype(jnp.bfloat16)
    returned = lax.all_to_all(
        replies.reshape(1, blocks_here, entry_count, width),
        "label",
        split_axis=2,
        concat_axis=0,
        tiled=True,
    )
    returned = returned.reshape(buffer_size, width)
    per_slot = jnp.where(
        present_flat[:, None],
        returned[jnp.minimum(slot_target, buffer_size - 1)],
        jnp.zeros((), jnp.bfloat16),
    )
    doc_grad = jnp.sum(
        per_slot.reshape(doc_total, beam_width, width).astype(jnp.float32), axis=1
    ).astype(jnp.bfloat16)
    partial_grad = jnp.einsum("bcj,bcd->bjd", coef, arrived, preferred_element_type=jnp.float32)
    label_grad = lax.psum_scatter(
        partial_grad.astype(jnp.bfloat16), "doc", scatter_dimension=1, tiled=True
    ).astype(jnp.float32)
    return (doc_grad, label_grad)


def solution(mesh):
    placed = (
        P(("parts", "label", "doc"), None),
        P("label", None),
        P(),
        P(("parts", "label"), None, None),
        P("parts"),
        P(("parts", "label", "doc"), None),
        P(("parts", "label", "doc"), None),
    )
    return jax.shard_map(
        local,
        mesh=mesh,
        in_specs=placed,
        out_specs=(P(("parts", "label", "doc"), None), P(("parts", "label"), "doc", None)),
        check_vma=False,
    )
```

profile of v0, /device:TPU:11, one launch (start us, length us, event | category | flops | bytes accessed | tf_op | source)
XLA Modules:
  0.0 114.7 jit_solution(17075202689971859304)
XLA Ops:
  7.2 0.0 copy-start
  7.2 0.0 all-gather.2.cloned.1.call-start
  7.2 0.7 all-gather.2.cloned.1.call-update
  7.9 0.7 broadcast_compare_fusion
  8.6 0.1 copy.59
  8.8 0.1 reshape.146
  8.9 0.1 broadcast_in_dim.90
  9.1 0.1 and.36
  9.2 0.7 select_multiply_fusion.1
  9.9 0.1 copy.61
  10.0 0.1 reshape.155
  10.2 1.9 %gather_fusion = s32[256]{0:T(256)S(1)} fusion(s32[64]{0:T(128)S(1)} %copy-done.1, s32[1024]{0:T(1024)S(1)} %pad_clamp_fusion.2), kind=kCustom, calls=%fused_computation | custom fusion | bytes 3072 | tf_op jit(solution)/shard_map/gather | solution.py:41
  12.1 0.6 reduce-window.6
  12.7 0.2 slice_reduce_fusion
  12.9 0.1 copy.65
  13.1 0.1 copy.66
  13.2 0.1 sub.34
  13.3 0.1 fusion.18
  13.5 0.1 and_select_fusion
  13.6 1.3 %scatter_custom_fusion = s32[512,5]{1,0:T(8,128)S(1)} fusion(s32[256]{0:T(256)S(1)} %bitcast.74, s32[256,4]{1,0:T(8,128)S(1)} %and_select_fusion, s32[]{:T(128)} %constant.23.clone.1, s32[]{:T(128)} %constant.17.clone.1), kind=kCustom, calls=%fused_computation.28 | custom fusion | bytes 141320 | tf_op jit(solution)/shard_map/scatter | solution.py:65
  15.0 0.4 copy.68
  15.4 0.8 reshape.217
  16.2 6.6 %all-to-all-start = ((s32[16,1,160]{2,1,0:T(1,128)}), s32[16,1,160]{2,1,0:T(1,128)S(1)}, u32[]{:S(2)}, u32[]{:S(2)}) async-start(s32[16,1,160]{2,1,0:T(1,128)} %reshape.217), calls=%async_computation | async-start | bytes 32768 | tf_op jit(solution)/shard_map/all_to_all | solution.py:70
  22.8 1.4 %scatter_custom_fusion.2 = s32[512]{0:T(512)S(1)} fusion(s32[256]{0:T(256)S(1)} %bitcast.75, s32[256]{0:T(256)S(1)} %and_select_fusion.1, s32[]{:T(128)} %constant.17.clone.1), kind=kCustom, calls=%fused_computation.57 | custom fusion | bytes 2052 | tf_op jit(solution)/shard_map/scatter | solution.py:52
  24.2 1.5 %scatter_custom_fusion.1 = pred[512]{0:T(512)(128)(4,1)S(1)} fusion(s32[256]{0:T(256)S(1)} %bitcast.76, pred[256]{0:T(512)(128)(4,1)S(1)} %broadcast.135, pred[]{:T(512)} %constant.24.clone.1), kind=kCustom, calls=%fused_computation.59 | custom fusion | bytes 513 | tf_op jit(solution)/shard_map/scatter | solution.py:54
  25.7 0.1 broadcast_in_dim.99
  25.8 23.0 %all-gather.2.cloned.1.call-done = bf16[768,768]{1,0:T(8,128)(2,1)} async-done(((bf16[48,768]{1,0:T(8,128)(2,1)}), bf16[768,768]{1,0:T(8,128)(2,1)}) %all-gather.2.cloned.1.call-update) | async-done | bytes 1179664 | tf_op jit(solution)/shard_map/all_gather | solution.py:29
  48.8 1.7 %multiply_reduce_fusion = (f32[128]{0:T(128)S(1)}, f32[128,768]{1,0:T(8,128)S(1)}) fusion(bf16[128,768]{1,0:T(8,128)(2,1)S(1)} %copy-done.2, bf16[768,768]{1,0:T(8,128)(2,1)} %all-gather.2.cloned.1.call-done), kind=kOutput, calls=%fused_computation.26 | convolution fusion | flops 151191424 | bytes 1769984 | tf_op jit(solution)/shard_map/dot_general | solution.py:27
  50.5 0.1 multiply_convert_fusion
  50.7 2.0 %gather_fusion.1 = bf16[512,768]{1,0:T(8,128)(2,1)S(1)} fusion(bf16[128,768]{1,0:T(8,128)(2,1)S(1)} %multiply_convert_fusion, s32[1024]{0:T(1024)S(1)} %pad_clamp_fusion.1), kind=kCustom, calls=%fused_computation.1 | custom fusion | bytes 1574912 | tf_op jit(solution)/shard_map/gather | solution.py:55
  52.7 1.0 broadcast_select_fusion
  53.7 5.4 %all-to-all-start.1 = ((bf16[16,4,8,768]{3,2,1,0:T(8,128)(2,1)}), bf16[16,4,8,768]{3,2,1,0:T(8,128)(2,1)S(1)}, u32[]{:S(2)}, u32[]{:S(2)}) async-start(bf16[16,4,8,768]{3,2,1,0:T(8,128)(2,1)} %broadcast_select_fusion), calls=%async_computation.1 | async-start | bytes 1572864 | tf_op jit(solution)/shard_map/all_to_all | solution.py:69
  59.1 0.5 broadcast.169
  59.6 0.7 reduce.3
  60.3 0.1 reshape.218
  60.5 0.1 reshape.149
  60.7 0.3 fusion.7
  61.0 17.3 %all-to-all-done.1 = bf16[16,4,8,768]{3,2,1,0:T(8,128)(2,1)S(1)} async-done(((bf16[16,4,8,768]{3,2,1,0:T(8,128)(2,1)}), bf16[16,4,8,768]{3,2,1,0:T(8,128)(2,1)S(1)}, u32[]{:S(2)}, u32[]{:S(2)}) %all-to-all-start.1) | async-done | bytes 786464 | tf_op jit(solution)/shard_map/all_to_all | solution.py:69
  78.4 0.4 fusion.6
  78.7 0.4 fusion.1
  79.1 1.5 %copy.72 = bf16[1,4,128,768]{3,1,0,2:T(4,128)(2,1)} copy(bf16[1,4,128,768]{3,2,1,0:T(8,128)(2,1)S(1)} %fusion.1) | data formatting | bytes 1572864 | tf_op jit(solution)/shard_map/reshape | solution.py:80
  80.6 5.0 %all-to-all-start.2 = ((bf16[1,4,128,768]{3,1,0,2:T(4,128)(2,1)}), bf16[1,4,128,768]{3,1,0,2:T(4,128)(2,1)S(1)}, u32[]{:S(2)}, u32[]{:S(2)}) async-start(bf16[1,4,128,768]{3,1,0,2:T(4,128)(2,1)} %copy.72), calls=%async_computation.2 | async-start | bytes 1572864 | tf_op jit(solution)/shard_map/all_to_all | solution.py:79
  85.6 1.6 %fusion = f32[4,128,768]{2,1,0:T(8,128)} fusion(bf16[4,128,128]{2,1,0:T(8,128)(2,1)S(1)} %fusion.6, bf16[16,4,8,768]{3,2,1,0:T(8,128)(2,1)S(1)} %all-to-all-done.1), kind=kOutput, calls=%fused_computation.7 | convolution fusion | flops 101449728 | bytes 2490368 | tf_op jit(solution)/shard_map/bcj,bcd->bjd/dot_general | solution.py:95
  87.1 17.7 %all-to-all-done.2 = bf16[1,4,128,768]{3,1,0,2:T(4,128)(2,1)S(1)} async-done(((bf16[1,4,128,768]{3,1,0,2:T(4,128)(2,1)}), bf16[1,4,128,768]{3,1,0,2:T(4,128)(2,1)S(1)}, u32[]{:S(2)}, u32[]{:S(2)}) %all-to-all-start.2) | async-done | bytes 786464 | tf_op jit(solution)/shard_map/all_to_all | solution.py:79
  104.8 0.1 copy.73
  104.9 1.2 %gather_fusion.2 = bf16[256,768]{1,0:T(8,128)(2,1)S(1)} fusion(bf16[512,768]{1,0:T(8,128)(2,1)S(1)} %bitcast.65, s32[1024]{0:T(1024)S(1)} %pad_clamp_fusion), kind=kCustom, calls=%fused_computation.2 | custom fusion | bytes 787456 | tf_op jit(solution)/shard_map/gather | solution.py:89
  106.1 0.2 gather.17
  106.2 1.6 %fusion.12 = bf16[128,768]{1,0:T(8,128)(2,1)} fusion(bf16[128,2,768]{2,1,0:T(2,128)(2,1)S(1)} %gather.17, pred[128,2]{1,0:T(8,128)(4,1)S(1)} %copy.59), kind=kLoop, calls=%fused_computation.24 | loop fusion | flops 294912 | bytes 590080 | tf_op jit(solution)/shard_map/reduce_sum | solution.py:92
  (28 shorter events, 0.2 us)
Async XLA Ops:
  7.2 71.2 %copy-start = (bf16[4,128,768]{2,1,0:T(8,128)(2,1)S(1)}, bf16[4,128,768]{2,1,0:T(8,128)(2,1)}, u32[]{:S(2)}) copy-start(bf16[4,128,768]{2,1,0:T(8,128)(2,1)} %param.10) | copy-start | bytes 2359300
  7.2 3.0 %copy-start.1 = (s32[64]{0:T(128)S(1)}, s32[64]{0:T(128)}, u32[]{:S(2)}) copy-start(s32[64]{0:T(128)} %param.11) | copy-start | bytes 772
  7.2 41.6 %all-gather.2.cloned.1.call-start = ((), (), s32[]{:S(2)}) async-start(), calls=%async_computation.3 | async-start | bytes 1253376 | tf_op jit(solution)/shard_map/all_gather | solution.py:29
  10.2 2.8 %copy-start.4 = (s32[128,4]{0,1:T(4,128)S(1)}, s32[128,4]{0,1:T(4,128)}, u32[]{:S(2)}) copy-start(s32[128,4]{0,1:T(4,128)} %param.13) | copy-start | bytes 6148
  12.1 36.8 %copy-start.2 = (bf16[128,768]{1,0:T(8,128)(2,1)S(1)}, bf16[128,768]{1,0:T(8,128)(2,1)}, u32[]{:S(2)}) copy-start(bf16[128,768]{1,0:T(8,128)(2,1)} %param.7) | copy-start | bytes 589828
  13.5 37.0 %copy-start.3 = (f32[768]{0:T(1024)S(1)}, f32[768]{0:T(1024)}, u32[]{:S(2)}) copy-start(f32[768]{0:T(1024)} %param.9) | copy-start | bytes 9220
  16.2 37.5 %all-to-all-start = ((s32[16,1,160]{2,1,0:T(1,128)}), s32[16,1,160]{2,1,0:T(1,128)S(1)}, u32[]{:S(2)}, u32[]{:S(2)}) async-start(s32[16,1,160]{2,1,0:T(1,128)} %reshape.217), calls=%async_computation | async-start | bytes 32768 | tf_op jit(solution)/shard_map/all_to_all | solution.py:70
  53.7 24.7 %all-to-all-start.1 = ((bf16[16,4,8,768]{3,2,1,0:T(8,128)(2,1)}), bf16[16,4,8,768]{3,2,1,0:T(8,128)(2,1)S(1)}, u32[]{:S(2)}, u32[]{:S(2)}) async-start(bf16[16,4,8,768]{3,2,1,0:T(8,128)(2,1)} %broadcast_select_fusion), calls=%async_computation.1 | async-start | bytes 1572864 | tf_op jit(solution)/shard_map/all_to_all | solution.py:69
  80.6 24.2 %all-to-all-start.2 = ((bf16[1,4,128,768]{3,1,0,2:T(4,128)(2,1)}), bf16[1,4,128,768]{3,1,0,2:T(4,128)(2,1)S(1)}, u32[]{:S(2)}, u32[]{:S(2)}) async-start(bf16[1,4,128,768]{3,1,0,2:T(4,128)(2,1)} %copy.72), calls=%async_computation.2 | async-start | bytes 1572864 | tf_op jit(solution)/shard_map/all_to_all | solution.py:79
Sparse Core Ops, SparseCore 0:
  10.3 38.4 all-gather.1
where the time goes:
time: 115 us
  waiting for transfers between devices  58.7 us (51%)
  starting transfers between devices  17 us (15%)
  local copies, waits for them, and re-layouts  14.6 us (13%)
  between operations  14.3 us (12%)
  other arithmetic  6.03 us (5%)
  matrix products  3.97 us (3%)
    all_gather x1, waiting for transfers between devices, local(): lax.all_gather(w_encoder, 'label', axis=0, tiled=True)  23 us
    all_to_all x1, waiting for transfers between devices, local(): lax.all_to_all(replies.reshape(1, blocks_here, entry_count, width), 'labe...  17.7 us
    all_to_all x1, waiting for transfers between devices, local(): lax.all_to_all(outgoing, 'label', split_axis=0, concat_axis=2, tiled=True)  17.3 us
    all_to_all x1, starting transfers between devices, local(): lax.all_to_all(info_buffer, 'label', split_axis=0, concat_axis=2, tiled=T...  6.55 us
    all_to_all x1, starting transfers between devices, local(): lax.all_to_all(outgoing, 'label', split_axis=0, concat_axis=2, tiled=True)  5.42 us
    all_to_all x1, starting transfers between devices, local(): lax.all_to_all(replies.reshape(1, blocks_here, entry_count, width), 'labe...  4.96 us
  transfers between devices with their start and end apart: 4, of which 3 were waited for; matrix products, arithmetic and copies ran while one was open for 17% of the time, Pallas kernels for 0%

commit v1 on v0

--- a/solution.py
+++ b/solution.py
@@ -1,9 +1,14 @@
+import functools
+
 import jax
 import jax.numpy as jnp
 from jax import lax
+from jax.experimental import pallas as pl
+from jax.experimental.pallas import tpu as pltpu
 from jax.sharding import PartitionSpec as P
 
 hinge_weight = 0.125
+BLOCK = 128
 
 
 def coefficients(entry_emb, entry_info, table_blocks):
@@ -99,6 +104,269 @@
     return (doc_grad, label_grad)
 
 
+MESH = pl.DeviceIdType.MESH
+META = 128
+
+
+def flipped(index, mask):
+    out = 0
+    place = 1
+    for _ in range(5):
+        out = out + ((index // place) % 2 + (mask // place) % 2) % 2 * place
+        place *= 2
+    return out
+
+
+def exchange_kernel(
+    shards, capacity,
+    feat_ref, w_ref, gain_ref, table_ref, place_ref, beams_ref, pos_ref,
+    doc_ref, lab_ref,
+    send_rows, arrived, w_all, embedded, coefs, replies, returned, pack,
+    w_send, w_recv, relay_send, f_send, f_recv, r_send, r_recv,
+):
+    me = lax.axis_index("label")
+    core = me % 2
+    chip = me // 2
+    partner = chip * 2 + 1 - core
+    chips = shards // 2
+    docs, width = feat_ref.shape
+    piece = w_ref.shape[0]
+    labels = table_ref.shape[0]
+    blocks_here = labels // BLOCK
+    slots = shards * capacity
+    total_blocks = place_ref.shape[1]
+
+    barrier = pltpu.get_barrier_semaphore()
+
+    @pl.loop(1, shards)
+    def _(t):
+        pl.semaphore_signal(barrier, inc=1, device_id={"label": flipped(me, t)}, device_id_type=MESH)
+
+    block_iota = lax.broadcasted_iota(jnp.int32, (docs, total_blocks), 1)
+    place = place_ref[...]
+
+    def row_of(block):
+        return jnp.sum(jnp.where(block == block_iota, place + 1, 0), axis=1, keepdims=True)
+
+    slot_iota = lax.broadcasted_iota(jnp.int32, (docs, slots), 1)
+    slot_shard = slot_iota // capacity
+    meta_iota = lax.broadcasted_iota(jnp.int32, (docs, META), 1)
+    meta = jnp.zeros((docs, META), jnp.int32)
+    hit = jnp.zeros((docs, slots), jnp.bool_)
+    beam_width = beams_ref.shape[1]
+    pos_total = pos_ref.shape[1]
+    for k in range(beam_width):
+        row = row_of(beams_ref[:, k : k + 1])
+        meta = jnp.where(meta_iota == k, row, meta)
+        target = jnp.where(row > 0, (row - 1) // blocks_here, -1)
+        hit = hit | (target == slot_shard)
+    for p in range(pos_total):
+        wanted = pos_ref[:, p : p + 1]
+        meta = jnp.where(meta_iota == beam_width + p, row_of(wanted // BLOCK), meta)
+        meta = jnp.where(meta_iota == beam_width + pos_total + p, wanted % BLOCK, meta)
+    hit_f = jnp.where(hit, 1.0, 0.0)
+    above = (
+        lax.broadcasted_iota(jnp.int32, (docs, docs), 0) > lax.broadcasted_iota(jnp.int32, (docs, docs), 1)
+    )
+    above = jnp.where(above, 1.0, 0.0).astype(jnp.bfloat16)
+    rank = jnp.dot(above, hit_f.astype(jnp.bfloat16), preferred_element_type=jnp.float32)
+    chosen = hit & (rank == (slot_iota % capacity).astype(jnp.float32))
+    pack[...] = jnp.where(chosen, 1.0, 0.0).astype(jnp.bfloat16)
+    over_docs = (((0,), (0,)), ((), ()))
+    send_rows[:, :width] = lax.dot_general(
+        pack[...], feat_ref[...], over_docs, preferred_element_type=jnp.float32
+    ).astype(jnp.bfloat16)
+    send_rows[:, width:] = lax.dot_general(
+        pack[...], meta.astype(jnp.float32).astype(jnp.bfloat16), over_docs,
+        preferred_element_type=jnp.float32,
+    ).astype(jnp.bfloat16)
+
+    def rows(index, size):
+        return pl.ds(pl.multiple_of(index * size, size), size)
+
+    def w_copy(owner, target, sem):
+        return pltpu.make_async_remote_copy(
+            src_ref=w_all.at[rows(owner, piece)], dst_ref=w_all.at[rows(owner, piece)],
+            send_sem=sem, recv_sem=w_recv.at[owner],
+            device_id={"label": target}, device_id_type=MESH,
+        )
+
+    def f_copy(target):
+        return pltpu.make_async_remote_copy(
+            src_ref=send_rows.at[rows(target, capacity)], dst_ref=arrived.at[rows(me, capacity)],
+            send_sem=f_send.at[target], recv_sem=f_recv.at[me],
+            device_id={"label": target}, device_id_type=MESH,
+        )
+
+    def f_arrival(source):
+        return pltpu.make_async_remote_copy(
+            src_ref=send_rows.at[rows(source, capacity)], dst_ref=arrived.at[rows(source, capacity)],
+            send_sem=f_send.at[source], recv_sem=f_recv.at[source],
+            device_id={"label": source}, device_id_type=MESH,
+        )
+
+    def r_copy(target):
+        return pltpu.make_async_remote_copy(
+            src_ref=replies.at[rows(target, capacity)], dst_ref=returned.at[rows(me, capacity)],
+            send_sem=r_send.at[target], recv_sem=r_recv.at[me],
+            device_id={"label": target}, device_id_type=MESH,
+        )
+
+    def r_arrival(source):
+        return pltpu.make_async_remote_copy(
+            src_ref=replies.at[rows(source, capacity)], dst_ref=returned.at[rows(source, capacity)],
+            send_sem=r_send.at[source], recv_sem=r_recv.at[source],
+            device_id={"label": source}, device_id_type=MESH,
+        )
+
+    w_all[rows(me, piece), :] = w_ref[...]
+    arrived[rows(me, capacity), :] = send_rows[rows(me, capacity), :]
+    pl.semaphore_wait(barrier, shards - 1)
+
+    @pl.loop(0, chips - 1)
+    def _(t):
+        other = flipped(chip, chips - 1 - t)
+        w_copy(me, other * 2 + core, w_send.at[other]).start()
+
+    w_copy(me, partner, w_send.at[chip]).start()
+
+    @pl.loop(0, shards - 1)
+    def _(t):
+        f_copy(flipped(me, shards - 1 - t)).start()
+
+    @pl.loop(1, chips)
+    def _(t):
+        other = flipped(chip, t)
+        owner = other * 2 + core
+        w_copy(owner, partner, relay_send.at[other]).wait_recv()
+        w_copy(owner, partner, relay_send.at[other]).start()
+
+    @pl.loop(0, chips)
+    def _(t):
+        owner = flipped(chip, t) * 2 + 1 - core
+        w_copy(owner, partner, w_send.at[chip]).wait_recv()
+
+    group = 4
+    chunk = group * capacity
+    column = lax.broadcasted_iota(jnp.int32, (chunk, labels), 1)
+    column_row = (column // BLOCK + me * blocks_here + 1).astype(jnp.float32)
+    column_key = (column + (me * blocks_here + 1) * BLOCK).astype(jnp.float32)
+
+    @pl.loop(0, shards // group)
+    def _(t):
+        plane = flipped(me // group, t)
+
+        @pl.loop(0, group)
+        def _(u):
+            source = plane * group + u
+
+            @pl.when(source != me)
+            def _():
+                f_arrival(source).wait_recv()
+
+        here = rows(plane, chunk)
+        encoded = jnp.dot(arrived[here, :width], w_all[...], preferred_element_type=jnp.float32)
+        scale = lax.rsqrt(jnp.mean(encoded * encoded, axis=-1, keepdims=True) + 1e-06)
+        emb = (encoded * scale * gain_ref[...]).astype(jnp.bfloat16)
+        embedded[here, :] = emb
+        info = arrived[here, width:].astype(jnp.float32)
+        scores = lax.dot_general(
+            emb, table_ref[...], (((1,), (1,)), ((), ())), preferred_element_type=jnp.float32
+        )
+        times = jnp.zeros((chunk, labels), jnp.float32)
+        for k in range(beam_width):
+            times = times + jnp.where(info[:, k : k + 1] == column_row, 1.0, 0.0)
+        signs = jnp.full((chunk, labels), -1.0, jnp.float32)
+        for p in range(pos_total):
+            a, b = beam_width + p, beam_width + pos_total + p
+            key = info[:, a : a + 1] * BLOCK + info[:, b : b + 1]
+            signs = jnp.where(key == column_key, 1.0, signs)
+        raw = -2.0 * hinge_weight * signs * jnp.maximum(0.0, 1.0 - signs * scores)
+        coef = jnp.where(times > 0.0, raw, 0.0).astype(jnp.bfloat16) * times.astype(jnp.bfloat16)
+        coefs[here, :] = coef
+        replies[here, :] = jnp.dot(
+            coef, table_ref[...], preferred_element_type=jnp.float32
+        ).astype(jnp.bfloat16)
+
+        @pl.loop(0, group)
+        def _(u):
+            source = plane * group + u
+
+            @pl.when(source != me)
+            def _():
+                r_copy(source).start()
+
+    returned[rows(me, capacity), :] = replies[rows(me, capacity), :]
+    for b in range(blocks_here):
+        lab_ref[b * BLOCK : (b + 1) * BLOCK, :] = lax.dot_general(
+            coefs[:, b * BLOCK : (b + 1) * BLOCK], embedded[...], over_docs,
+            preferred_element_type=jnp.float32,
+        )
+
+    @pl.loop(1, shards)
+    def _(t):
+        r_arrival(flipped(me, t)).wait_recv()
+
+    doc_ref[...] = jnp.dot(
+        pack[...], returned[...], preferred_element_type=jnp.float32
+    ).astype(jnp.bfloat16)
+
+    @pl.loop(1, shards)
+    def _(t):
+        other = flipped(me, t)
+        f_copy(other).wait_send()
+        r_copy(other).wait_send()
+
+    @pl.loop(0, chips)
+    def _(t):
+        w_copy(me, partner, w_send.at[t]).wait_send()
+
+    @pl.loop(1, chips)
+    def _(t):
+        w_copy(me, partner, relay_send.at[flipped(chip, t)]).wait_send()
+
+
+def local_fused(features, w_encoder, norm_gain, label_table, block_place, beams, positives):
+    docs, width = features.shape
+    blocks_here, block_size, _ = label_table.shape
+    shards = lax.axis_size("label")
+    slot_total = docs * beams.shape[1]
+    per_block = max(2, 2 * slot_total // (blocks_here * shards))
+    capacity = blocks_here * per_block
+    labels = blocks_here * block_size
+    slots = shards * capacity
+    vmem = pl.BlockSpec(memory_space=pltpu.VMEM)
+    dma = pltpu.SemaphoreType.DMA
+    doc_grad, label_grad = pl.pallas_call(
+        functools.partial(exchange_kernel, shards, capacity),
+        out_shape=(
+            jax.ShapeDtypeStruct((docs, width), jnp.bfloat16),
+            jax.ShapeDtypeStruct((labels, width), jnp.float32),
+        ),
+        in_specs=[vmem] * 7,
+        out_specs=(vmem, vmem),
+        scratch_shapes=[
+            pltpu.VMEM((slots, width + META), jnp.bfloat16),
+            pltpu.VMEM((slots, width + META), jnp.bfloat16),
+            pltpu.VMEM((width, width), jnp.bfloat16),
+            pltpu.VMEM((slots, width), jnp.bfloat16),
+            pltpu.VMEM((slots, labels), jnp.bfloat16),
+            pltpu.VMEM((slots, width), jnp.bfloat16),
+            pltpu.VMEM((slots, width), jnp.bfloat16),
+            pltpu.VMEM((docs, slots), jnp.bfloat16),
+            dma((shards // 2,)), dma((shards,)), dma((shards // 2,)),
+            dma((shards,)), dma((shards,)), dma((shards,)), dma((shards,)),
+        ],
+        compiler_params=pltpu.CompilerParams(
+            collective_id=0, has_side_effects=True, vmem_limit_bytes=40 * 1024 * 1024
+        ),
+    )(
+        features, w_encoder, norm_gain.reshape(1, width), label_table.reshape(labels, width),
+        block_place.reshape(1, -1), beams, positives,
+    )
+    return doc_grad, label_grad.reshape(blocks_here, block_size, width)
+
+
 def solution(mesh):
     placed = (
         P(("parts", "label", "doc"), None),
@@ -109,8 +377,9 @@
         P(("parts", "label", "doc"), None),
         P(("parts", "label", "doc"), None),
     )
+    one_kernel = mesh.shape["doc"] == 1 and mesh.shape["label"] == 16
     return jax.shard_map(
-        local,
+        local_fused if one_kernel else local,
         mesh=mesh,
         in_specs=placed,
         out_specs=(P(("parts", "label", "doc"), None), P(("parts", "label"), "doc", None)),

time: 115 us -> 65.5 us (0.57)
  waiting for transfers between devices: 58.7 us -> 0 us
  Pallas kernels: 0 us -> 56.9 us
  starting transfers between devices: 17 us -> 0 us
  between operations: 14.3 us -> 0.65 us
  local copies, waits for them, and re-layouts: 14.6 us -> 7.68 us
  other arithmetic: 6.03 us -> 0 us
  matrix products: 3.97 us -> 0 us
    pallas_call x0 -> x1, Pallas kernels: none -> 56.9 us  [local_fused(): pl.pallas_call(functools.partial(exchange_kernel, shards, capacity), out_...]
    all_to_all x3 -> x0, waiting for transfers between devices: 35 us -> none  [the longest x1 17.7 us: local(): lax.all_to_all(replies.reshape(1, blocks_here, entry_count, width), 'labe...]
    all_gather x1 -> x0, waiting for transfers between devices: 23 us -> none  [local(): lax.all_gather(w_encoder, 'label', axis=0, tiled=True)]
    all_to_all x3 -> x0, starting transfers between devices: 16.9 us -> none  [the longest x1 6.55 us: local(): lax.all_to_all(info_buffer, 'label', split_axis=0, concat_axis=2, tiled=T...]
    unnamed x13 -> x12, local copies, waits for them, and re-layouts: 1.07 us -> 6.99 us
    gather x4 -> x0, local copies, waits for them, and re-layouts: 5.23 us -> none  [the longest x1 2.03 us: local(): embedded[source_docs]]
    scatter x3 -> x0, local copies, waits for them, and re-layouts: 4.2 us -> none  [the longest x1 1.49 us: local(): jnp.zeros((buffer_size,), jnp.bool_).at[slot_target].set(True, mode='drop')]
    dot_general x4 -> x0, matrix products: 3.97 us -> none  [the longest x1 1.68 us: local(): jnp.dot(features, lax.all_gather(w_encoder, 'label', axis=0, tiled=True),...]
  transfers between devices with their start and end apart: 4 -> 0, of which waited for: 3 -> 0; matrix products, arithmetic and copies ran while one was open for 17% -> 0% of each run, Pallas kernels for 0% -> 0%
where the time goes in v1:
time: 65.5 us; the launch traced here: 65.2 us
  Pallas kernels  56.9 us (87%)
  local copies, waits for them, and re-layouts  7.68 us (12%)
    pallas_call x1, Pallas kernels, local_fused(): pl.pallas_call(functools.partial(exchange_kernel, shards, capacity), out_...  56.9 us
    unnamed x12, local copies, waits for them, and re-layouts  6.99 us

profile of v1, /device:TPU:11, one launch (start us, length us, event | category | flops | bytes accessed | tf_op | source)
XLA Modules:
  0.0 65.2 jit_solution(7321409031603112679)
XLA Ops:
  0.6 0.7 %reshape.16.gain_ref = f32[1,768]{1,0:T(1,128)S(1)} reshape(f32[768]{0:T(1024)} %param.9) | data formatting | bytes 6144 | tf_op jit(solution)/shard_map/reshape | solution.py:364
  1.3 0.8 %copy.9.beams_ref = s32[128,2]{1,0:T(8,128)S(1)} copy(s32[128,2]{0,1:T(2,128)} %param.12) | data formatting | bytes 2048 | tf_op args[5]
  2.1 0.8 %copy.10.pos_ref = s32[128,4]{1,0:T(8,128)S(1)} copy(s32[128,4]{0,1:T(4,128)} %param.13) | data formatting | bytes 4096 | tf_op args[6]
  2.9 0.0 copy-start
  2.9 1.1 %copy-done = bf16[4,128,768]{2,1,0:T(8,128)(2,1)S(1)} copy-done((bf16[4,128,768]{2,1,0:T(8,128)(2,1)S(1)}, bf16[4,128,768]{2,1,0:T(8,128)(2,1)}, u32[]{:S(2)}) %copy-start) | copy-done | bytes 786456
  4.0 0.0 copy-start.1
  4.0 0.9 %copy-done.1 = bf16[128,768]{1,0:T(8,128)(2,1)S(1)} copy-done((bf16[128,768]{1,0:T(8,128)(2,1)S(1)}, bf16[128,768]{1,0:T(8,128)(2,1)}, u32[]{:S(2)}) %copy-start.1) | copy-done | bytes 196632
  5.0 0.0 copy-start.2
  5.0 0.9 %copy-done.2 = bf16[48,768]{1,0:T(8,128)(2,1)S(1)} copy-done((bf16[48,768]{1,0:T(8,128)(2,1)S(1)}, bf16[48,768]{1,0:T(8,128)(2,1)}, u32[]{:S(2)}) %copy-start.2) | copy-done | bytes 73752
  5.8 0.0 copy-start.3
  5.8 0.7 %copy-done.3 = s32[64]{0:T(128)S(1)} copy-done((s32[64]{0:T(128)S(1)}, s32[64]{0:T(128)}, u32[]{:S(2)}) %copy-start.3) | copy-done | bytes 280
  6.5 56.9 %shard_map.86 = (bf16[128,768]{1,0:T(8,128)(2,1)S(1)}, f32[512,768]{1,0:T(8,128)S(1)}) custom-call(bf16[128,768]{1,0:T(8,128)(2,1)S(1)} %copy-done.1, bf16[48,768]{1,0:T(8,128)(2,1)S(1)} %copy-done.2, f32[1,768]{1,0:T(1,128)S(1)} %reshape.16.gain_ref, bf16[512,768]{1,0:T(8,128)(2,1)S(1)} %bitcast.4, s32[1,64]{1,0:T(1,128)S(1)} %bitcast.5, ...), custom_call_target="tpu_custom_call" | custom-call | tf_op jit(solution)/shard_map/pallas_call | solution.py:340
  63.4 0.7 %copy.13 = bf16[128,768]{1,0:T(8,128)(2,1)} copy(bf16[128,768]{1,0:T(8,128)(2,1)S(1)} %get-tuple-element.8) | data formatting | bytes 393216
  64.1 1.1 %copy.14 = f32[4,128,768]{2,1,0:T(8,128)} copy(f32[4,128,768]{2,1,0:T(8,128)S(1)} %bitcast.3) | data formatting | bytes 3145728
Async XLA Ops:
  2.9 1.1 %copy-start = (bf16[4,128,768]{2,1,0:T(8,128)(2,1)S(1)}, bf16[4,128,768]{2,1,0:T(8,128)(2,1)}, u32[]{:S(2)}) copy-start(bf16[4,128,768]{2,1,0:T(8,128)(2,1)} %param.10) | copy-start | bytes 2359300
  4.0 0.9 %copy-start.1 = (bf16[128,768]{1,0:T(8,128)(2,1)S(1)}, bf16[128,768]{1,0:T(8,128)(2,1)}, u32[]{:S(2)}) copy-start(bf16[128,768]{1,0:T(8,128)(2,1)} %feat_ref.1) | copy-start | bytes 589828
  5.0 0.9 %copy-start.2 = (bf16[48,768]{1,0:T(8,128)(2,1)S(1)}, bf16[48,768]{1,0:T(8,128)(2,1)}, u32[]{:S(2)}) copy-start(bf16[48,768]{1,0:T(8,128)(2,1)} %w_ref.1) | copy-start | bytes 221188
  5.8 0.7 %copy-start.3 = (s32[64]{0:T(128)S(1)}, s32[64]{0:T(128)}, u32[]{:S(2)}) copy-start(s32[64]{0:T(128)} %param.11) | copy-start | bytes 772

commit v2 on v1

--- a/solution.py
+++ b/solution.py
@@ -9,6 +9,7 @@
 
 hinge_weight = 0.125
 BLOCK = 128
+LANES = 128
 
 
 def coefficients(entry_emb, entry_info, table_blocks):
@@ -119,22 +120,30 @@
 
 def exchange_kernel(
     shards, capacity,
-    feat_ref, w_ref, gain_ref, table_ref, place_ref, beams_ref, pos_ref,
+    feat_hbm, w_hbm, gain_hbm, table_hbm, place_hbm, beams_hbm, pos_hbm,
     doc_ref, lab_ref,
+    feat_ref, gain_ref, table_ref, place_ref, beams_ref, pos_ref,
     send_rows, arrived, w_all, embedded, coefs, replies, returned, pack,
-    w_send, w_recv, relay_send, f_send, f_recv, r_send, r_recv,
+    load, wz_send, wx_send, wp_send, w_recv, f_send, f_recv, r_send, r_recv,
 ):
     me = lax.axis_index("label")
     core = me % 2
-    chip = me // 2
-    partner = chip * 2 + 1 - core
-    chips = shards // 2
+    cross = me // 2 % 2
+    level = me // 4
+    levels = shards // 4
+    partner = me + 1 - 2 * core
+    beside = me + 2 - 4 * cross
     docs, width = feat_ref.shape
-    piece = w_ref.shape[0]
+    piece = w_hbm.shape[0]
     labels = table_ref.shape[0]
     blocks_here = labels // BLOCK
     slots = shards * capacity
     total_blocks = place_ref.shape[1]
+    beam_width = beams_ref.shape[0]
+    pos_total = pos_ref.shape[0]
+
+    def rows(index, size):
+        return pl.ds(pl.multiple_of(index * size, size), size)
 
     barrier = pltpu.get_barrier_semaphore()
 
@@ -142,47 +151,55 @@
     def _(t):
         pl.semaphore_signal(barrier, inc=1, device_id={"label": flipped(me, t)}, device_id_type=MESH)
 
-    block_iota = lax.broadcasted_iota(jnp.int32, (docs, total_blocks), 1)
-    place = place_ref[...]
+    loads = [
+        pltpu.make_async_copy(src, dst, load.at[i])
+        for i, (src, dst) in enumerate((
+            (beams_hbm, beams_ref), (place_hbm, place_ref), (pos_hbm, pos_ref), (feat_hbm, feat_ref),
+            (w_hbm, w_all.at[rows(me, piece)]), (gain_hbm, gain_ref), (table_hbm, table_ref),
+        ))
+    ]
+    for one in loads:
+        one.start()
+    for one in loads[:4]:
+        one.wait()
+
+    block_iota = lax.broadcasted_iota(jnp.int32, (total_blocks, docs), 0)
+    place = (place_ref[...] + 1).astype(jnp.float32).astype(jnp.bfloat16)
 
     def row_of(block):
-        return jnp.sum(jnp.where(block == block_iota, place + 1, 0), axis=1, keepdims=True)
-
-    slot_iota = lax.broadcasted_iota(jnp.int32, (docs, slots), 1)
+        at = jnp.where(block == block_iota, 1.0, 0.0).astype(jnp.bfloat16)
+        return jnp.dot(place, at, preferred_element_type=jnp.float32).astype(jnp.int32)
+
+    slot_iota = lax.broadcasted_iota(jnp.int32, (slots, docs), 0)
     slot_shard = slot_iota // capacity
-    meta_iota = lax.broadcasted_iota(jnp.int32, (docs, META), 1)
-    meta = jnp.zeros((docs, META), jnp.int32)
-    hit = jnp.zeros((docs, slots), jnp.bool_)
-    beam_width = beams_ref.shape[1]
-    pos_total = pos_ref.shape[1]
+    meta_iota = lax.broadcasted_iota(jnp.int32, (META, docs), 0)
+    meta = jnp.zeros((META, docs), jnp.int32)
+    hit = jnp.zeros((slots, docs), jnp.bool_)
     for k in range(beam_width):
-        row = row_of(beams_ref[:, k : k + 1])
+        row = row_of(beams_ref[k : k + 1, :])
         meta = jnp.where(meta_iota == k, row, meta)
         target = jnp.where(row > 0, (row - 1) // blocks_here, -1)
         hit = hit | (target == slot_shard)
     for p in range(pos_total):
-        wanted = pos_ref[:, p : p + 1]
+        wanted = pos_ref[p : p + 1, :]
         meta = jnp.where(meta_iota == beam_width + p, row_of(wanted // BLOCK), meta)
         meta = jnp.where(meta_iota == beam_width + pos_total + p, wanted % BLOCK, meta)
     hit_f = jnp.where(hit, 1.0, 0.0)
-    above = (
-        lax.broadcasted_iota(jnp.int32, (docs, docs), 0) > lax.broadcasted_iota(jnp.int32, (docs, docs), 1)
-    )
-    above = jnp.where(above, 1.0, 0.0).astype(jnp.bfloat16)
-    rank = jnp.dot(above, hit_f.astype(jnp.bfloat16), preferred_element_type=jnp.float32)
+    before = (
+        lax.broadcasted_iota(jnp.int32, (docs, docs), 0) < lax.broadcasted_iota(jnp.int32, (docs, docs), 1)
+    )
+    before = jnp.where(before, 1.0, 0.0).astype(jnp.bfloat16)
+    rank = jnp.dot(hit_f.astype(jnp.bfloat16), before, preferred_element_type=jnp.float32)
     chosen = hit & (rank == (slot_iota % capacity).astype(jnp.float32))
     pack[...] = jnp.where(chosen, 1.0, 0.0).astype(jnp.bfloat16)
     over_docs = (((0,), (0,)), ((), ()))
-    send_rows[:, :width] = lax.dot_general(
-        pack[...], feat_ref[...], over_docs, preferred_element_type=jnp.float32
+    send_rows[:, :width] = jnp.dot(
+        pack[...], feat_ref[...], preferred_element_type=jnp.float32
     ).astype(jnp.bfloat16)
     send_rows[:, width:] = lax.dot_general(
-        pack[...], meta.astype(jnp.float32).astype(jnp.bfloat16), over_docs,
+        pack[...], meta.astype(jnp.float32).astype(jnp.bfloat16), (((1,), (1,)), ((), ())),
         preferred_element_type=jnp.float32,
     ).astype(jnp.bfloat16)
-
-    def rows(index, size):
-        return pl.ds(pl.multiple_of(index * size, size), size)
 
     def w_copy(owner, target, sem):
         return pltpu.make_async_remote_copy(
@@ -191,61 +208,94 @@
             device_id={"label": target}, device_id_type=MESH,
         )
 
-    def f_copy(target):
+    def slot_copy(out, into, send, recv, target, source):
         return pltpu.make_async_remote_copy(
-            src_ref=send_rows.at[rows(target, capacity)], dst_ref=arrived.at[rows(me, capacity)],
-            send_sem=f_send.at[target], recv_sem=f_recv.at[me],
+            src_ref=out.at[rows(target, capacity)], dst_ref=into.at[rows(source, capacity)],
+            send_sem=send.at[target], recv_sem=recv.at[source],
             device_id={"label": target}, device_id_type=MESH,
         )
 
+    def f_copy(target):
+        return slot_copy(send_rows, arrived, f_send, f_recv, target, me)
+
     def f_arrival(source):
-        return pltpu.make_async_remote_copy(
-            src_ref=send_rows.at[rows(source, capacity)], dst_ref=arrived.at[rows(source, capacity)],
-            send_sem=f_send.at[source], recv_sem=f_recv.at[source],
-            device_id={"label": source}, device_id_type=MESH,
-        )
+        return slot_copy(send_rows, arrived, f_send, f_recv, source, source)
 
     def r_copy(target):
-        return pltpu.make_async_remote_copy(
-            src_ref=replies.at[rows(target, capacity)], dst_ref=returned.at[rows(me, capacity)],
-            send_sem=r_send.at[target], recv_sem=r_recv.at[me],
-            device_id={"label": target}, device_id_type=MESH,
-        )
+        return slot_copy(replies, returned, r_send, r_recv, target, me)
 
     def r_arrival(source):
-        return pltpu.make_async_remote_copy(
-            src_ref=replies.at[rows(source, capacity)], dst_ref=returned.at[rows(source, capacity)],
-            send_sem=r_send.at[source], recv_sem=r_recv.at[source],
-            device_id={"label": source}, device_id_type=MESH,
-        )
-
-    w_all[rows(me, piece), :] = w_ref[...]
+        return slot_copy(replies, returned, r_send, r_recv, source, source)
+
     arrived[rows(me, capacity), :] = send_rows[rows(me, capacity), :]
+    loads[4].wait()
     pl.semaphore_wait(barrier, shards - 1)
 
-    @pl.loop(0, chips - 1)
-    def _(t):
-        other = flipped(chip, chips - 1 - t)
-        w_copy(me, other * 2 + core, w_send.at[other]).start()
-
-    w_copy(me, partner, w_send.at[chip]).start()
-
-    @pl.loop(0, shards - 1)
-    def _(t):
-        f_copy(flipped(me, shards - 1 - t)).start()
-
-    @pl.loop(1, chips)
-    def _(t):
-        other = flipped(chip, t)
-        owner = other * 2 + core
-        w_copy(owner, partner, relay_send.at[other]).wait_recv()
-        w_copy(owner, partner, relay_send.at[other]).start()
-
-    @pl.loop(0, chips)
-    def _(t):
-        owner = flipped(chip, t) * 2 + 1 - core
-        w_copy(owner, partner, w_send.at[chip]).wait_recv()
-
+    same = cross * 2 + core
+
+    def pass_on(z):
+        w_copy(z * 4 + same, beside, wx_send.at[z]).start()
+        w_copy(z * 4 + same, partner, wp_send.at[z * 2 + cross]).start()
+
+    def features_to(t):
+        plane = flipped(level, t)
+
+        @pl.loop(0, 4)
+        def _(u):
+            target = plane * 4 + flipped(u, same)
+
+            @pl.when(target != me)
+            def _():
+                f_copy(target).start()
+
+    for s in range(levels):
+        if s < levels - 1:
+            @pl.when((level >= s) & (level < levels - 1))
+            def _():
+                if s:
+                    w_copy(me - 4 * s, partner, wz_send.at[0]).wait_recv()
+                w_copy(me - 4 * s, me + 4, wz_send.at[s]).start()
+
+            @pl.when((level + s < levels) & (level > 0))
+            def _():
+                if s:
+                    w_copy(me + 4 * s, partner, wz_send.at[0]).wait_recv()
+                w_copy(me + 4 * s, me - 4, wz_send.at[levels + s]).start()
+
+        if s:
+            @pl.when((level >= s) & ((level == levels - 1) | (s == levels - 1)))
+            def _():
+                w_copy(me - 4 * s, partner, wz_send.at[0]).wait_recv()
+
+            @pl.when((level + s < levels) & ((level == 0) | (s == levels - 1)))
+            def _():
+                w_copy(me + 4 * s, partner, wz_send.at[0]).wait_recv()
+
+            @pl.when(level >= s)
+            def _():
+                pass_on(level - s)
+
+            @pl.when(level + s < levels)
+            def _():
+                pass_on(level + s)
+        else:
+            pass_on(level)
+        features_to(levels - 1 - s)
+
+    @pl.loop(0, levels)
+    def _(t):
+        z = flipped(level, t)
+        owner = z * 4 + (1 - cross) * 2 + core
+        w_copy(owner, partner, wz_send.at[0]).wait_recv()
+        w_copy(owner, partner, wp_send.at[z * 2 + 1 - cross]).start()
+
+    @pl.loop(0, shards // 2)
+    def _(t):
+        w_copy(t * 2 + 1 - core, partner, wz_send.at[0]).wait_recv()
+
+    loads[5].wait()
+    loads[6].wait()
+    gain = jnp.concatenate([gain_ref[i : i + 1, :] for i in range(width // LANES)], axis=1)
     group = 4
     chunk = group * capacity
     column = lax.broadcasted_iota(jnp.int32, (chunk, labels), 1)
@@ -254,7 +304,7 @@
 
     @pl.loop(0, shards // group)
     def _(t):
-        plane = flipped(me // group, t)
+        plane = flipped(level, levels - 1 - t)
 
         @pl.loop(0, group)
         def _(u):
@@ -267,7 +317,7 @@
         here = rows(plane, chunk)
         encoded = jnp.dot(arrived[here, :width], w_all[...], preferred_element_type=jnp.float32)
         scale = lax.rsqrt(jnp.mean(encoded * encoded, axis=-1, keepdims=True) + 1e-06)
-        emb = (encoded * scale * gain_ref[...]).astype(jnp.bfloat16)
+        emb = (encoded * scale * gain).astype(jnp.bfloat16)
         embedded[here, :] = emb
         info = arrived[here, width:].astype(jnp.float32)
         scores = lax.dot_general(
@@ -307,8 +357,8 @@
     def _(t):
         r_arrival(flipped(me, t)).wait_recv()
 
-    doc_ref[...] = jnp.dot(
-        pack[...], returned[...], preferred_element_type=jnp.float32
+    doc_ref[...] = lax.dot_general(
+        pack[...], returned[...], over_docs, preferred_element_type=jnp.float32
     ).astype(jnp.bfloat16)
 
     @pl.loop(1, shards)
@@ -317,13 +367,22 @@
         f_copy(other).wait_send()
         r_copy(other).wait_send()
 
-    @pl.loop(0, chips)
-    def _(t):
-        w_copy(me, partner, w_send.at[t]).wait_send()
-
-    @pl.loop(1, chips)
-    def _(t):
-        w_copy(me, partner, relay_send.at[flipped(chip, t)]).wait_send()
+    for s in range(levels - 1):
+        @pl.when((level >= s) & (level < levels - 1))
+        def _():
+            w_copy(me, partner, wz_send.at[s]).wait_send()
+
+        @pl.when((level + s < levels) & (level > 0))
+        def _():
+            w_copy(me, partner, wz_send.at[levels + s]).wait_send()
+
+    @pl.loop(0, levels)
+    def _(t):
+        w_copy(me, partner, wx_send.at[t]).wait_send()
+
+    @pl.loop(0, shards // 2)
+    def _(t):
+        w_copy(me, partner, wp_send.at[t]).wait_send()
 
 
 def local_fused(features, w_encoder, norm_gain, label_table, block_place, beams, positives):
@@ -343,9 +402,15 @@
             jax.ShapeDtypeStruct((docs, width), jnp.bfloat16),
             jax.ShapeDtypeStruct((labels, width), jnp.float32),
         ),
-        in_specs=[vmem] * 7,
+        in_specs=[pl.BlockSpec(memory_space=pl.ANY)] * 7,
         out_specs=(vmem, vmem),
         scratch_shapes=[
+            pltpu.VMEM((docs, width), jnp.bfloat16),
+            pltpu.VMEM((width // LANES, LANES), jnp.float32),
+            pltpu.VMEM((labels, width), jnp.bfloat16),
+            pltpu.VMEM((1, block_place.shape[0]), jnp.int32),
+            pltpu.VMEM((beams.shape[1], docs), jnp.int32),
+            pltpu.VMEM((positives.shape[1], docs), jnp.int32),
             pltpu.VMEM((slots, width + META), jnp.bfloat16),
             pltpu.VMEM((slots, width + META), jnp.bfloat16),
             pltpu.VMEM((width, width), jnp.bfloat16),
@@ -353,16 +418,16 @@
             pltpu.VMEM((slots, labels), jnp.bfloat16),
             pltpu.VMEM((slots, width), jnp.bfloat16),
             pltpu.VMEM((slots, width), jnp.bfloat16),
-            pltpu.VMEM((docs, slots), jnp.bfloat16),
-            dma((shards // 2,)), dma((shards,)), dma((shards // 2,)),
+            pltpu.VMEM((slots, docs), jnp.bfloat16),
+            dma((7,)), dma((shards // 2,)), dma((shards // 4,)), dma((shards // 2,)), dma((shards,)),
             dma((shards,)), dma((shards,)), dma((shards,)), dma((shards,)),
         ],
         compiler_params=pltpu.CompilerParams(
-            collective_id=0, has_side_effects=True, vmem_limit_bytes=40 * 1024 * 1024
+            collective_id=0, has_side_effects=True, vmem_limit_bytes=60 * 1024 * 1024
         ),
     )(
-        features, w_encoder, norm_gain.reshape(1, width), label_table.reshape(labels, width),
-        block_place.reshape(1, -1), beams, positives,
+        features, w_encoder, norm_gain.reshape(-1, LANES), label_table.reshape(labels, width),
+        block_place.reshape(1, -1), beams.T, positives.T,
     )
     return doc_grad, label_grad.reshape(blocks_here, block_size, width)
 

time: 65.5 us -> 66 us (level)
  Pallas kernels: 56.9 us -> 60.9 us
  local copies, waits for them, and re-layouts: 7.68 us -> 4.31 us
    pallas_call x1, Pallas kernels: 56.9 us -> 60.9 us  [local_fused(): pl.pallas_call(functools.partial(exchange_kernel, shards, capacity), out_...]
    unnamed x12 -> x2, local copies, waits for them, and re-layouts: 6.99 us -> 4.31 us
    reshape x1 -> x0, local copies, waits for them, and re-layouts: 0.69 us -> none  [local_fused(): norm_gain.reshape(1, width)]
where the time goes in v2:
time: 66 us; the launch traced here: 65.8 us
  Pallas kernels  60.9 us (92%)
  local copies, waits for them, and re-layouts  4.31 us (7%)
    pallas_call x1, Pallas kernels, local_fused(): pl.pallas_call(functools.partial(exchange_kernel, shards, capacity), out_...  60.9 us
    unnamed x2, local copies, waits for them, and re-layouts  4.31 us

profile of v2, /device:TPU:11, one launch (start us, length us, event | category | flops | bytes accessed | tf_op | source)
XLA Modules:
  0.0 65.8 jit_solution(2353344979264384402)
XLA Ops:
  0.6 60.9 %shard_map.86 = (bf16[128,768]{1,0:T(8,128)(2,1)}, f32[512,768]{1,0:T(8,128)}) custom-call(bf16[128,768]{1,0:T(8,128)(2,1)} %feat_hbm.1, bf16[48,768]{1,0:T(8,128)(2,1)} %w_hbm.1, f32[6,128]{1,0:T(8,128)} %bitcast.8, bf16[512,768]{1,0:T(8,128)(2,1)} %bitcast.7, s32[1,64]{1,0:T(1,128)} %bitcast.11, s32[2,128]{1,0:T(2,128)} %bitcast.10, s32[4,128]{1,0:T(4,128)} %bitcast.9), custom_call_target="tpu_custom_call" | custom-call | tf_op jit(solution)/shard_map/pallas_call | solution.py:399
  61.5 1.6 %copy.11 = bf16[128,768]{1,0:T(8,128)(2,1)} copy(bf16[128,768]{1,0:T(8,128)(2,1)} %get-tuple-element.8) | data formatting | bytes 393216
  63.1 2.7 %copy.12 = f32[4,128,768]{2,1,0:T(8,128)} copy(f32[4,128,768]{2,1,0:T(8,128)} %bitcast.6) | data formatting | bytes 3145728

commit v3 on v2

--- a/solution.py
+++ b/solution.py
@@ -110,26 +110,27 @@
 
 
 def flipped(index, mask):
-    out = 0
     place = 1
-    for _ in range(5):
-        out = out + ((index // place) % 2 + (mask // place) % 2) % 2 * place
+    while place <= mask:
+        if mask // place % 2:
+            bit = lax.rem(lax.div(index, place), 2)
+            index = index + (1 - 2 * bit) * place
         place *= 2
-    return out
+    return index
 
 
 def exchange_kernel(
     shards, capacity,
     feat_hbm, w_hbm, gain_hbm, table_hbm, place_hbm, beams_hbm, pos_hbm,
-    doc_ref, lab_ref,
+    doc_ref, coefs, embedded,
     feat_ref, gain_ref, table_ref, place_ref, beams_ref, pos_ref,
-    send_rows, arrived, w_all, embedded, coefs, replies, returned, pack,
+    send_rows, arrived, w_all, replies, returned, pack,
     load, wz_send, wx_send, wp_send, w_recv, f_send, f_recv, r_send, r_recv,
 ):
     me = lax.axis_index("label")
-    core = me % 2
-    cross = me // 2 % 2
-    level = me // 4
+    core = lax.rem(me, 2)
+    cross = lax.rem(lax.div(me, 2), 2)
+    level = lax.div(me, 4)
     levels = shards // 4
     partner = me + 1 - 2 * core
     beside = me + 2 - 4 * cross
@@ -149,7 +150,7 @@
 
     @pl.loop(1, shards)
     def _(t):
-        pl.semaphore_signal(barrier, inc=1, device_id={"label": flipped(me, t)}, device_id_type=MESH)
+        pl.semaphore_signal(barrier, inc=1, device_id={"label": lax.rem(me + t, shards)}, device_id_type=MESH)
 
     loads = [
         pltpu.make_async_copy(src, dst, load.at[i])
@@ -160,6 +161,58 @@
     ]
     for one in loads:
         one.start()
+    def w_copy(owner, target, sem):
+        return pltpu.make_async_remote_copy(
+            src_ref=w_all.at[rows(owner, piece)], dst_ref=w_all.at[rows(owner, piece)],
+            send_sem=sem, recv_sem=w_recv.at[owner],
+            device_id={"label": target}, device_id_type=MESH,
+        )
+
+    def slot_copy(out, into, send, recv, target, source):
+        return pltpu.make_async_remote_copy(
+            src_ref=out.at[rows(target, capacity)], dst_ref=into.at[rows(source, capacity)],
+            send_sem=send.at[target], recv_sem=recv.at[source],
+            device_id={"label": target}, device_id_type=MESH,
+        )
+
+    def f_copy(target):
+        return slot_copy(send_rows, arrived, f_send, f_recv, target, me)
+
+    def f_arrival(source):
+        return slot_copy(send_rows, arrived, f_send, f_recv, source, source)
+
+    def r_copy(target):
+        return slot_copy(replies, returned, r_send, r_recv, target, me)
+
+    def r_arrival(source):
+        return slot_copy(replies, returned, r_send, r_recv, source, source)
+
+    same = cross * 2 + core
+
+    def pass_on(z):
+        w_copy(z * 4 + same, beside, wx_send.at[z]).start()
+        w_copy(z * 4 + same, partner, wp_send.at[z * 2 + cross]).start()
+
+    def features_to(t):
+        plane = flipped(level, t)
+
+        @pl.loop(0, 4)
+        def _(u):
+            target = plane * 4 + u
+
+            @pl.when(target != me)
+            def _():
+                f_copy(target).start()
+
+    loads[4].wait()
+    pl.semaphore_wait(barrier, shards - 1)
+
+    for t in range(1, levels):
+        other = flipped(level, levels - t)
+        w_copy(me, other * 4 + same, wz_send.at[other]).start()
+
+    pass_on(level)
+
     for one in loads[:4]:
         one.wait()
 
@@ -201,97 +254,29 @@
         preferred_element_type=jnp.float32,
     ).astype(jnp.bfloat16)
 
-    def w_copy(owner, target, sem):
-        return pltpu.make_async_remote_copy(
-            src_ref=w_all.at[rows(owner, piece)], dst_ref=w_all.at[rows(owner, piece)],
-            send_sem=sem, recv_sem=w_recv.at[owner],
-            device_id={"label": target}, device_id_type=MESH,
-        )
-
-    def slot_copy(out, into, send, recv, target, source):
-        return pltpu.make_async_remote_copy(
-            src_ref=out.at[rows(target, capacity)], dst_ref=into.at[rows(source, capacity)],
-            send_sem=send.at[target], recv_sem=recv.at[source],
-            device_id={"label": target}, device_id_type=MESH,
-        )
-
-    def f_copy(target):
-        return slot_copy(send_rows, arrived, f_send, f_recv, target, me)
-
-    def f_arrival(source):
-        return slot_copy(send_rows, arrived, f_send, f_recv, source, source)
-
-    def r_copy(target):
-        return slot_copy(replies, returned, r_send, r_recv, target, me)
-
-    def r_arrival(source):
-        return slot_copy(replies, returned, r_send, r_recv, source, source)
-
     arrived[rows(me, capacity), :] = send_rows[rows(me, capacity), :]
-    loads[4].wait()
-    pl.semaphore_wait(barrier, shards - 1)
-
-    same = cross * 2 + core
-
-    def pass_on(z):
-        w_copy(z * 4 + same, beside, wx_send.at[z]).start()
-        w_copy(z * 4 + same, partner, wp_send.at[z * 2 + cross]).start()
-
-    def features_to(t):
-        plane = flipped(level, t)
-
-        @pl.loop(0, 4)
-        def _(u):
-            target = plane * 4 + flipped(u, same)
-
-            @pl.when(target != me)
-            def _():
-                f_copy(target).start()
-
-    for s in range(levels):
-        if s < levels - 1:
-            @pl.when((level >= s) & (level < levels - 1))
-            def _():
-                if s:
-                    w_copy(me - 4 * s, partner, wz_send.at[0]).wait_recv()
-                w_copy(me - 4 * s, me + 4, wz_send.at[s]).start()
-
-            @pl.when((level + s < levels) & (level > 0))
-            def _():
-                if s:
-                    w_copy(me + 4 * s, partner, wz_send.at[0]).wait_recv()
-                w_copy(me + 4 * s, me - 4, wz_send.at[levels + s]).start()
-
-        if s:
-            @pl.when((level >= s) & ((level == levels - 1) | (s == levels - 1)))
-            def _():
-                w_copy(me - 4 * s, partner, wz_send.at[0]).wait_recv()
-
-            @pl.when((level + s < levels) & ((level == 0) | (s == levels - 1)))
-            def _():
-                w_copy(me + 4 * s, partner, wz_send.at[0]).wait_recv()
-
-            @pl.when(level >= s)
-            def _():
-                pass_on(level - s)
-
-            @pl.when(level + s < levels)
-            def _():
-                pass_on(level + s)
-        else:
-            pass_on(level)
-        features_to(levels - 1 - s)
-
-    @pl.loop(0, levels)
-    def _(t):
+
+    for t in (3, 2):
+        features_to(t)
+
+    for t in range(1, levels):
+        z = flipped(level, t)
+        w_copy(z * 4 + same, partner, wz_send.at[0]).wait_recv()
+        pass_on(z)
+
+    for t in range(0, levels):
         z = flipped(level, t)
         owner = z * 4 + (1 - cross) * 2 + core
         w_copy(owner, partner, wz_send.at[0]).wait_recv()
         w_copy(owner, partner, wp_send.at[z * 2 + 1 - cross]).start()
 
+    for t in (1, 0):
+        features_to(t)
+
     @pl.loop(0, shards // 2)
     def _(t):
         w_copy(t * 2 + 1 - core, partner, wz_send.at[0]).wait_recv()
+
 
     loads[5].wait()
     loads[6].wait()
@@ -304,7 +289,8 @@
 
     @pl.loop(0, shards // group)
     def _(t):
-        plane = flipped(level, levels - 1 - t)
+        high, low = lax.div(level, 2), lax.rem(level, 2)
+        plane = jnp.where(t < 2, 1 - high, high) * 2 + jnp.where(lax.rem(t, 2) == 0, 1 - low, low)
 
         @pl.loop(0, group)
         def _(u):
@@ -347,15 +333,9 @@
                 r_copy(source).start()
 
     returned[rows(me, capacity), :] = replies[rows(me, capacity), :]
-    for b in range(blocks_here):
-        lab_ref[b * BLOCK : (b + 1) * BLOCK, :] = lax.dot_general(
-            coefs[:, b * BLOCK : (b + 1) * BLOCK], embedded[...], over_docs,
-            preferred_element_type=jnp.float32,
-        )
-
     @pl.loop(1, shards)
     def _(t):
-        r_arrival(flipped(me, t)).wait_recv()
+        r_arrival(lax.rem(me + t, shards)).wait_recv()
 
     doc_ref[...] = lax.dot_general(
         pack[...], returned[...], over_docs, preferred_element_type=jnp.float32
@@ -363,21 +343,14 @@
 
     @pl.loop(1, shards)
     def _(t):
-        other = flipped(me, t)
+        other = lax.rem(me + t, shards)
         f_copy(other).wait_send()
         r_copy(other).wait_send()
 
-    for s in range(levels - 1):
-        @pl.when((level >= s) & (level < levels - 1))
-        def _():
-            w_copy(me, partner, wz_send.at[s]).wait_send()
-
-        @pl.when((level + s < levels) & (level > 0))
-        def _():
-            w_copy(me, partner, wz_send.at[levels + s]).wait_send()
-
-    @pl.loop(0, levels)
-    def _(t):
+    for t in range(1, levels):
+        w_copy(me, partner, wz_send.at[flipped(level, t)]).wait_send()
+
+    for t in range(0, levels):
         w_copy(me, partner, wx_send.at[t]).wait_send()
 
     @pl.loop(0, shards // 2)
@@ -396,14 +369,15 @@
     slots = shards * capacity
     vmem = pl.BlockSpec(memory_space=pltpu.VMEM)
     dma = pltpu.SemaphoreType.DMA
-    doc_grad, label_grad = pl.pallas_call(
+    doc_grad, coefs, embedded = pl.pallas_call(
         functools.partial(exchange_kernel, shards, capacity),
         out_shape=(
             jax.ShapeDtypeStruct((docs, width), jnp.bfloat16),
-            jax.ShapeDtypeStruct((labels, width), jnp.float32),
+            jax.ShapeDtypeStruct((slots, labels), jnp.bfloat16),
+            jax.ShapeDtypeStruct((slots, width), jnp.bfloat16),
         ),
         in_specs=[pl.BlockSpec(memory_space=pl.ANY)] * 7,
-        out_specs=(vmem, vmem),
+        out_specs=(vmem, vmem, vmem),
         scratch_shapes=[
             pltpu.VMEM((docs, width), jnp.bfloat16),
             pltpu.VMEM((width // LANES, LANES), jnp.float32),
@@ -414,8 +388,6 @@
             pltpu.VMEM((slots, width + META), jnp.bfloat16),
             pltpu.VMEM((slots, width + META), jnp.bfloat16),
             pltpu.VMEM((width, width), jnp.bfloat16),
-            pltpu.VMEM((slots, width), jnp.bfloat16),
-            pltpu.VMEM((slots, labels), jnp.bfloat16),
             pltpu.VMEM((slots, width), jnp.bfloat16),
             pltpu.VMEM((slots, width), jnp.bfloat16),
             pltpu.VMEM((slots, docs), jnp.bfloat16),
@@ -429,6 +401,9 @@
         features, w_encoder, norm_gain.reshape(-1, LANES), label_table.reshape(labels, width),
         block_place.reshape(1, -1), beams.T, positives.T,
     )
+    label_grad = lax.dot_general(
+        coefs, embedded, (((0,), (0,)), ((), ())), preferred_element_type=jnp.float32
+    )
     return doc_grad, label_grad.reshape(blocks_here, block_size, width)
 
 

time: 66 us -> 56.7 us (0.86)
  the two profiles are of different devices: /device:TPU:11 before, /device:TPU:0 now
where the time goes in v3:
time: 56.7 us; the launch traced here: 56.5 us
  Pallas kernels  52.1 us (92%)
  matrix products  3.07 us (5%)
  local copies, waits for them, and re-layouts  0.68 us (1%)
  between operations  0.65 us (1%)
    pallas_call x1, Pallas kernels, local_fused(): pl.pallas_call(functools.partial(exchange_kernel, shards, capacity), out_...  52.1 us
    dot_general x1, matrix products, local_fused(): lax.dot_general(coefs, embedded, (((0,), (0,)), ((), ())), preferred_elem...  3.07 us

profile of v3, /device:TPU:0, one launch (start us, length us, event | category | flops | bytes accessed | tf_op | source)
XLA Modules:
  0.0 56.5 jit_solution(1602884934492460040)
XLA Ops:
  0.6 52.1 %shard_map.86 = (bf16[128,768]{1,0:T(8,128)(2,1)}, bf16[512,512]{1,0:T(8,128)(2,1)}, bf16[512,768]{1,0:T(8,128)(2,1)}) custom-call(bf16[128,768]{1,0:T(8,128)(2,1)} %feat_hbm.1, bf16[48,768]{1,0:T(8,128)(2,1)} %w_hbm.1, f32[6,128]{1,0:T(8,128)} %bitcast.10, bf16[512,768]{1,0:T(8,128)(2,1)} %bitcast.9, s32[1,64]{1,0:T(1,128)} %bitcast.13, s32[2,128]{1,0:T(2,128)} %bitcast.12, ...), custom_call_target="tpu_custom_call" | custom-call | tf_op jit(solution)/shard_map/pallas_call | solution.py:372
  52.7 0.0 copy-start
  52.7 3.1 %fusion = f32[512,768]{1,0:T(8,128)} fusion(bf16[512,512]{1,0:T(8,128)(2,1)} %get-tuple-element.6, bf16[512,768]{1,0:T(8,128)(2,1)} %get-tuple-element.7), kind=kOutput, calls=%fused_computation | convolution fusion | flops 402653184 | bytes 2883584 | tf_op jit(solution)/shard_map/dot_general | solution.py:404
  55.8 0.0 copy-done
  55.8 0.7 %copy.10 = bf16[128,768]{1,0:T(8,128)(2,1)} copy(bf16[128,768]{1,0:T(8,128)(2,1)S(1)} %copy-done) | data formatting | bytes 393216
Async XLA Ops:
  52.7 3.1 %copy-start = (bf16[128,768]{1,0:T(8,128)(2,1)S(1)}, bf16[128,768]{1,0:T(8,128)(2,1)}, u32[]{:S(2)}) copy-start(bf16[128,768]{1,0:T(8,128)(2,1)} %get-tuple-element.10) | copy-start | bytes 589828

commit v4 on v3

--- a/solution.py
+++ b/solution.py
@@ -106,7 +106,7 @@
 
 
 MESH = pl.DeviceIdType.MESH
-META = 128
+META = 16
 
 
 def flipped(index, mask):
@@ -125,7 +125,7 @@
     doc_ref, coefs, embedded,
     feat_ref, gain_ref, table_ref, place_ref, beams_ref, pos_ref,
     send_rows, arrived, w_all, replies, returned, pack,
-    load, wz_send, wx_send, wp_send, w_recv, f_send, f_recv, r_send, r_recv,
+    load, wz_send, wx_send, wp_send, w_recv, f_send, f_recv, r_send, r_recv, m_send, m_recv, m_out, m_in,
 ):
     me = lax.axis_index("label")
     core = lax.rem(me, 2)
@@ -181,6 +181,13 @@
     def f_arrival(source):
         return slot_copy(send_rows, arrived, f_send, f_recv, source, source)
 
+    def m_copy(target, source):
+        return pltpu.make_async_remote_copy(
+            src_ref=m_out.at[rows(lax.div(target, 4), META)], dst_ref=m_in.at[rows(source, META)],
+            send_sem=m_send.at[target], recv_sem=m_recv.at[source],
+            device_id={"label": target}, device_id_type=MESH,
+        )
+
     def r_copy(target):
         return slot_copy(replies, returned, r_send, r_recv, target, me)
 
@@ -202,6 +209,7 @@
 
             @pl.when(target != me)
             def _():
+                m_copy(target, me).start()
                 f_copy(target).start()
 
     loads[4].wait()
@@ -246,14 +254,17 @@
     chosen = hit & (rank == (slot_iota % capacity).astype(jnp.float32))
     pack[...] = jnp.where(chosen, 1.0, 0.0).astype(jnp.bfloat16)
     over_docs = (((0,), (0,)), ((), ()))
-    send_rows[:, :width] = jnp.dot(
+    send_rows[...] = jnp.dot(
         pack[...], feat_ref[...], preferred_element_type=jnp.float32
     ).astype(jnp.bfloat16)
-    send_rows[:, width:] = lax.dot_general(
-        pack[...], meta.astype(jnp.float32).astype(jnp.bfloat16), (((1,), (1,)), ((), ())),
+    packed = lax.dot_general(
+        meta.astype(jnp.float32).astype(jnp.bfloat16), pack[...], (((1,), (1,)), ((), ())),
         preferred_element_type=jnp.float32,
     ).astype(jnp.bfloat16)
-
+    span = 4 * capacity
+    for z in range(levels):
+        m_out[z * META : (z + 1) * META, :] = packed[:, z * span : (z + 1) * span]
+    m_in[rows(me, META), :] = m_out[rows(level, META), :]
     arrived[rows(me, capacity), :] = send_rows[rows(me, capacity), :]
 
     for t in (3, 2):
@@ -282,6 +293,9 @@
     loads[6].wait()
     gain = jnp.concatenate([gain_ref[i : i + 1, :] for i in range(width // LANES)], axis=1)
     group = 4
+    at = lax.broadcasted_iota(jnp.int32, (capacity, group * capacity), 1)
+    own_slot = lax.broadcasted_iota(jnp.int32, (capacity, group * capacity), 0) + same * capacity
+    mine = jnp.where(at == own_slot, 1.0, 0.0).astype(jnp.bfloat16)
     chunk = group * capacity
     column = lax.broadcasted_iota(jnp.int32, (chunk, labels), 1)
     column_row = (column // BLOCK + me * blocks_here + 1).astype(jnp.float32)
@@ -299,13 +313,18 @@
             @pl.when(source != me)
             def _():
                 f_arrival(source).wait_recv()
+                m_copy(source, source).wait_recv()
 
         here = rows(plane, chunk)
-        encoded = jnp.dot(arrived[here, :width], w_all[...], preferred_element_type=jnp.float32)
+        encoded = jnp.dot(arrived[here, :], w_all[...], preferred_element_type=jnp.float32)
         scale = lax.rsqrt(jnp.mean(encoded * encoded, axis=-1, keepdims=True) + 1e-06)
         emb = (encoded * scale * gain).astype(jnp.bfloat16)
         embedded[here, :] = emb
-        info = arrived[here, width:].astype(jnp.float32)
+        fields = lax.dot_general(
+            mine, m_in[rows(plane, group * META), :], (((1,), (1,)), ((), ())),
+            preferred_element_type=jnp.float32,
+        )
+        info = jnp.concatenate([fields[:, i * META : (i + 1) * META] for i in range(group)], axis=0)
         scores = lax.dot_general(
             emb, table_ref[...], (((1,), (1,)), ((), ())), preferred_element_type=jnp.float32
         )
@@ -345,6 +364,7 @@
     def _(t):
         other = lax.rem(me + t, shards)
         f_copy(other).wait_send()
+        m_copy(other, me).wait_send()
         r_copy(other).wait_send()
 
     for t in range(1, levels):
@@ -385,14 +405,16 @@
             pltpu.VMEM((1, block_place.shape[0]), jnp.int32),
             pltpu.VMEM((beams.shape[1], docs), jnp.int32),
             pltpu.VMEM((positives.shape[1], docs), jnp.int32),
-            pltpu.VMEM((slots, width + META), jnp.bfloat16),
-            pltpu.VMEM((slots, width + META), jnp.bfloat16),
+            pltpu.VMEM((slots, width), jnp.bfloat16),
+            pltpu.VMEM((slots, width), jnp.bfloat16),
             pltpu.VMEM((width, width), jnp.bfloat16),
             pltpu.VMEM((slots, width), jnp.bfloat16),
             pltpu.VMEM((slots, width), jnp.bfloat16),
             pltpu.VMEM((slots, docs), jnp.bfloat16),
             dma((7,)), dma((shards // 2,)), dma((shards // 4,)), dma((shards // 2,)), dma((shards,)),
-            dma((shards,)), dma((shards,)), dma((shards,)), dma((shards,)),
+            dma((shards,)), dma((shards,)), dma((shards,)), dma((shards,)), dma((shards,)), dma((shards,)),
+            pltpu.VMEM((shards // 4 * META, LANES), jnp.bfloat16),
+            pltpu.VMEM((shards * META, LANES), jnp.bfloat16),
         ],
         compiler_params=pltpu.CompilerParams(
             collective_id=0, has_side_effects=True, vmem_limit_bytes=60 * 1024 * 1024

time: 56.7 us -> 55.4 us (0.977)
  the two profiles are of different devices: /device:TPU:0 before, /device:TPU:3 now
where the time goes in v4:
time: 55.4 us; the launch traced here: 55.2 us
  Pallas kernels  50.8 us (92%)
  matrix products  3.07 us (6%)
  local copies, waits for them, and re-layouts  0.68 us (1%)
  between operations  0.65 us (1%)
    pallas_call x1, Pallas kernels, local_fused(): pl.pallas_call(functools.partial(exchange_kernel, shards, capacity), out_...  50.8 us
    dot_general x1, matrix products, local_fused(): lax.dot_general(coefs, embedded, (((0,), (0,)), ((), ())), preferred_elem...  3.07 us

profile of v4, /device:TPU:3, one launch (start us, length us, event | category | flops | bytes accessed | tf_op | source)
XLA Modules:
  0.0 55.2 jit_solution(9043903285465445761)
XLA Ops:
  0.6 50.8 %shard_map.86 = (bf16[128,768]{1,0:T(8,128)(2,1)}, bf16[512,512]{1,0:T(8,128)(2,1)}, bf16[512,768]{1,0:T(8,128)(2,1)}) custom-call(bf16[128,768]{1,0:T(8,128)(2,1)} %feat_hbm.1, bf16[48,768]{1,0:T(8,128)(2,1)} %w_hbm.1, f32[6,128]{1,0:T(8,128)} %bitcast.10, bf16[512,768]{1,0:T(8,128)(2,1)} %bitcast.9, s32[1,64]{1,0:T(1,128)} %bitcast.13, s32[2,128]{1,0:T(2,128)} %bitcast.12, ...), custom_call_target="tpu_custom_call" | custom-call | tf_op jit(solution)/shard_map/pallas_call | solution.py:392
  51.5 0.0 copy-start
  51.5 3.1 %fusion = f32[512,768]{1,0:T(8,128)} fusion(bf16[512,512]{1,0:T(8,128)(2,1)} %get-tuple-element.6, bf16[512,768]{1,0:T(8,128)(2,1)} %get-tuple-element.7), kind=kOutput, calls=%fused_computation | convolution fusion | flops 402653184 | bytes 2883584 | tf_op jit(solution)/shard_map/dot_general | solution.py:426
  54.6 0.0 copy-done
  54.6 0.7 %copy.10 = bf16[128,768]{1,0:T(8,128)(2,1)} copy(bf16[128,768]{1,0:T(8,128)(2,1)S(1)} %copy-done) | data formatting | bytes 393216
Async XLA Ops:
  51.5 3.1 %copy-start = (bf16[128,768]{1,0:T(8,128)(2,1)S(1)}, bf16[128,768]{1,0:T(8,128)(2,1)}, u32[]{:S(2)}) copy-start(bf16[128,768]{1,0:T(8,128)(2,1)} %get-tuple-element.10) | copy-start | bytes 589828
